TPU v7x, 256 devices: a whole 4x4x8 slice. The times are simulated.
256 devices in a mesh: row: 16 (over x, y_hi, core), col: 16 (over y_lo, z).
Axes of the slice: x: 4, y: 4 (y_hi: 2, y_lo: 2; y = y_hi * 2 + y_lo), z: 8, core: 2. Of those that a mesh axis runs over, the one named last changes fastest.
Arguments:
- matrix: float32 [16, 3, 256, 16, 3, 256], P('row', None, None, 'col'), as said below
- checksum: float32 [16, 3, 256, 3, 256], P('row'), as said below
- failed: int32 [16], P('col'), may hold values from 0 to 15, as said below
Outputs:
- factored: float32 [16, 3, 256, 16, 3, 256], P('row', None, None, 'col')
- updated_checksum_result: float32 [16, 3, 256, 3, 256], P('row')
Inputs may be any that keep to these rules, and one draw needn't show every extreme that they name: `failed`: a permutation of the grid column indices; entry 0 names the grid column whose tiles in matrix carry no information. With the lost grid column rebuilt from checksum, matrix is symmetric positive definite. `checksum`: for each grid row, the sum over all grid columns of the intact matrix's tiles, the lost column included.
All inputs are finite; a program needn't handle non-finite values.
Results may differ from a plain program's by a relative error of at most 0.0003.
Values sent between devices are 32-bit elements; how exact they have to be, the bound alone decides.
No kernel may reach another device: no remote copies, remote signals or barrier semaphores. Data moves between devices by JAX's collectives and lax.ppermute only.
A program may use at most 128 MiB of HBM per device.

v0:
```python
import jax
import jax.numpy as jnp
from jax import lax
from jax.experimental import pallas as pl
from jax.experimental.pallas import tpu as pltpu
from jax.sharding import Mesh
from jax.sharding import PartitionSpec as P

PANELS = 3
ROW = ("xy", "core")
COL = ("col_0", "col_1")
LOWER = [(0, 0), (1, 0), (1, 1), (2, 0), (2, 1), (2, 2)]
F32 = jnp.float32
VMEM = pl.BlockSpec(memory_space=pltpu.VMEM)
SMEM = pl.BlockSpec(memory_space=pltpu.SMEM)


def mm(a, b):
    return lax.dot_general(
        a, b, (((1,), (0,)), ((), ())), precision=lax.Precision.HIGHEST, preferred_element_type=F32
    )


def mm_t(a, b):
    return lax.dot_general(
        a, b, (((1,), (1,)), ((), ())), precision=lax.Precision.HIGHEST, preferred_element_type=F32
    )


def halves(x):
    high = x.astype(jnp.bfloat16)
    return high, (x - high.astype(F32)).astype(jnp.bfloat16)


def high_twice(x, axis):
    high, low = halves(x)
    return jnp.concatenate([high, high, low], axis)


def low_between(x, axis):
    high, low = halves(x)
    return jnp.concatenate([high, low, high], axis)


def dot3(a, b):
    return lax.dot_general(a, b, (((1,), (0,)), ((), ())), preferred_element_type=F32)


def dot3_t(a, b):
    return lax.dot_general(a, b, (((1,), (1,)), ((), ())), preferred_element_type=F32)


def base_inverse(a):
    n = a.shape[0]
    groups = n // 8
    rows = lax.broadcasted_iota(jnp.int32, (8, n), 0)
    lanes = lax.broadcasted_iota(jnp.int32, (8, n), 1)
    ag = [a[8 * g : 8 * g + 8, :] for g in range(groups)]
    mg = [jnp.where(lanes == rows + 8 * g, 1.0, 0.0).astype(F32) for g in range(groups)]
    for m in range(groups):
        columns = [
            [
                jnp.broadcast_to(ag[g][:, 8 * m + k : 8 * m + k + 1], (8, n))
                for g in range(m, groups)
            ]
            for k in range(8)
        ]
        top, mine = ag[m], mg[m]
        us, vs, ls = [], [], []
        for k in range(8):
            scale = lax.rsqrt(columns[k][0][k : k + 1, :])
            l = [x * scale for x in columns[k]]
            for k2 in range(k + 1, 8):
                s = l[0][k2 : k2 + 1, :]
                columns[k2] = [x - y * s for x, y in zip(columns[k2], l)]
            u = top[k : k + 1, :] * scale
            v = mine[k : k + 1, :] * scale
            below = jnp.where(rows > k, l[0], 0.0)
            top = top - below * u
            mine = jnp.where(rows == k, v, mine - below * v)
            us.append(u)
            vs.append(v)
            ls.append(l[1:])
        mg[m] = mine
        for t, g in enumerate(range(m + 1, groups)):
            ag[g] = ag[g] - sum(ls[k][t] * us[k] for k in range(8))
            mg[g] = mg[g] - sum(ls[k][t] * vs[k] for k in range(8))
    return jnp.concatenate(mg, axis=0)


def tile_inverse(a):
    h = a.shape[0] // 2
    first = base_inverse(a[:h, :h])
    l10 = mm_t(a[h:, :h], first)
    second = base_inverse(a[h:, h:] - mm_t(l10, l10))
    low = -mm(second, mm(l10, first))
    return jnp.concatenate(
        [
            jnp.concatenate([first, jnp.zeros_like(first)], 1),
            jnp.concatenate([low, second], 1),
        ],
        0,
    )


def whole(ref, n):
    t = ref[:, n]
    return t.reshape(t.shape[0] * t.shape[1], t.shape[2])


def woven(even, odd, n):
    t = jnp.stack([even[:, n], odd[:, n]], axis=1)
    return t.reshape(256, 256)


def by_core(core, mine_ref, other_ref, body):
    @pl.when(core == 0)
    def _():
        body(mine_ref, other_ref)

    @pl.when(core != 0)
    def _():
        body(other_ref, mine_ref)


def lead_kernel(core_ref, mine_ref, other_ref, off_ref, inv_ref, t_ref):
    def gather(even, odd):
        for n in range(6):
            t_ref[n] = woven(even, odd, n)

    by_core(core_ref[0], mine_ref, other_ref, gather)
    i0 = tile_inverse(t_ref[0])
    inv_ref[0] = i0
    l10 = mm_t(t_ref[1], i0)
    off_ref[0] = l10
    i1 = tile_inverse(t_ref[2] - mm_t(l10, l10))
    inv_ref[1] = i1
    l20 = mm_t(t_ref[3], i0)
    off_ref[1] = l20
    l21 = mm_t(t_ref[4] - mm_t(l20, l10), i1)
    off_ref[2] = l21
    inv_ref[2] = tile_inverse(t_ref[5] - mm_t(l20, l20) - mm_t(l21, l21))


def tile_rows(a, b, half):
    return pl.ds(a * 1536 + 2 * b + half, 256, stride=6)


def prepare_kernel(m_ref, f_ref, col_ref):
    for n, (a, b) in enumerate(LOWER):
        for half in range(2):
            v = m_ref[tile_rows(a, b, half), :].reshape(16, 16, 128)
            col_ref[:, 16 * n : 16 * n + 16, 128 * half : 128 * half + 128] = v
    col_ref[:, 96:104, :] = jnp.full((16, 8, 256), f_ref[0].astype(F32))


def rebuild_kernel(g_ref, c_ref, panel_ref, lost_ref, send_ref):
    missing = g_ref[0, 96:97, :]
    for n, (a, b) in enumerate(LOWER):
        part = slice(16 * n, 16 * n + 16)
        healthy = jnp.zeros((16, 256), F32)
        for j in range(16):
            healthy = healthy + jnp.where(missing != float(j), g_ref[j, part, :], 0.0)
        rebuilt = c_ref[a, b] - healthy
        lost_ref[n] = rebuilt
        if b == 0:
            for k in range(PANELS):
                v = jnp.where(missing == float(k), rebuilt, g_ref[k, part, :])
                panel_ref[3 * a + k] = v
                if a == 0:
                    for s in range(16):
                        send_ref[s, k] = v


def lead_half_kernel(core_ref, g_ref, send_ref):
    rows = pl.ds(pl.multiple_of(8 * core_ref[0], 8), 8)
    for n, (i, k) in enumerate(LOWER):
        v = g_ref[i, k, rows, :]
        for s in range(16):
            send_ref[s, n] = v


def solve_kernel(
    core_ref, r_ref, mine_ref, other_ref, c_ref, off_ref, inv_ref,
    t_ref, x_ref, x3_ref, y3_ref, q_ref, k_ref, s3_ref, w3_ref,
):

    def gather(even, odd):
        for n in range(9):
            q_ref[n] = woven(even, odd, n)
            k_ref[n] = woven(even, odd, 9 + n)

    by_core(core_ref[0], mine_ref, other_ref, gather)

    for k in range(PANELS):
        w3_ref[k] = low_between(inv_ref[k], 1)
        w3_ref[3 + k] = low_between(off_ref[k], 1)

    def solve(tile):
        x0 = dot3_t(high_twice(tile(0), 1), w3_ref[0])
        x0_3 = high_twice(x0, 1)
        x1 = dot3_t(high_twice(tile(1) - dot3_t(x0_3, w3_ref[3]), 1), w3_ref[1])
        x1_3 = high_twice(x1, 1)
        rest = tile(2) - dot3_t(x0_3, w3_ref[4]) - dot3_t(x1_3, w3_ref[5])
        x2 = dot3_t(high_twice(rest, 1), w3_ref[2])
        return (x0, x1, x2), (x0_3, x1_3)

    @pl.loop(0, 3)
    def _(a):
        xs, (x0_3, x1_3) = solve(lambda k: whole(r_ref, 3 * a + k))
        for k in range(PANELS):
            x_ref[a, k] = xs[k]
        x3_ref[a, :, 0:768] = x0_3
        x3_ref[a, :, 768:1536] = x1_3
        x3_ref[a, :, 1536:2304] = high_twice(xs[2], 1)

    @pl.loop(0, 3)
    def _(b):
        ys, _ = solve(lambda k: q_ref[3 * b + k])
        for k in range(PANELS):
            y3_ref[b, :, 768 * k : 768 * k + 768] = low_between(ys[k], 1)

    @pl.loop(0, 3)
    def _(b):
        s0 = dot3(w3_ref[0], high_twice(k_ref[b], 0))
        s3_ref[b, 0:768] = low_between(s0, 0)
        s0_3 = high_twice(s0, 0)
        s1 = dot3(w3_ref[1], high_twice(k_ref[3 + b] - dot3(w3_ref[3], s0_3), 0))
        s3_ref[b, 768:1536] = low_between(s1, 0)
        s1_3 = high_twice(s1, 0)
        rest = k_ref[6 + b] - dot3(w3_ref[4], s0_3) - dot3(w3_ref[5], s1_3)
        s2 = dot3(w3_ref[2], high_twice(rest, 0))
        s3_ref[b, 1536:2304] = low_between(s2, 0)

    @pl.loop(0, 9)
    def _(n):
        a, b = n // 3, n % 3
        t_ref[a, b] = c_ref[a, b] - dot3(x3_ref[a], s3_ref[b])


def finish_kernel(place_ref, d_ref, m_ref, x_ref, x3_ref, y3_ref, f_ref):
    p, q, missing = place_ref[0], place_ref[1], place_ref[2]

    def store(a, b, value):
        for half in range(2):
            f_ref[tile_rows(a, b, half), :] = value[:, 128 * half : 128 * half + 128]

    for n, (a, b) in enumerate(LOWER):
        i, j = p + 16 * a, q + 16 * b
        kept = i >= j
        panel = jnp.logical_and(kept, j < PANELS) if b == 0 else jnp.bool_(False)
        inner = jnp.logical_and(kept, jnp.logical_not(panel))

        @pl.when(jnp.logical_not(kept))
        def _():
            store(a, b, jnp.zeros((256, 256), F32))

        if b == 0:

            @pl.when(panel)
            def _():
                value = x_ref[a, jnp.minimum(q, PANELS - 1)]
                rows = lax.broadcasted_iota(jnp.int32, (256, 256), 0)
                cols = lax.broadcasted_iota(jnp.int32, (256, 256), 1)
                value = jnp.where(jnp.logical_or(rows >= cols, i > q), value, 0.0)
                store(a, b, value)

        @pl.when(inner)
        def _():
            update = dot3_t(x3_ref[a], y3_ref[b])

            @pl.when(q == missing)
            def _():
                store(a, b, whole(d_ref, n) - update)

            @pl.when(q != missing)
            def _():
                for half in range(2):
                    rows = tile_rows(a, b, half)
                    f_ref[rows, :] = m_ref[rows, :] - update[:, 128 * half : 128 * half + 128]

    for a, b in ((0, 1), (0, 2), (1, 2)):
        store(a, b, jnp.zeros((256, 256), F32))


def call(
    kernel, outs, ins, specs=None, scratch=(), flops=10**6,
    halves_outs=(), halves_scratch=(), limit=16,
):
    shapes = [jax.ShapeDtypeStruct(s, F32) for s in outs]
    shapes += [jax.ShapeDtypeStruct(s, jnp.bfloat16) for s in halves_outs]
    return pl.pallas_call(
        kernel,
        out_shape=shapes,
        in_specs=specs or [VMEM] * len(ins),
        out_specs=[VMEM] * len(shapes),
        scratch_shapes=[pltpu.VMEM(s, F32) for s in scratch]
        + [pltpu.VMEM(s, jnp.bfloat16) for s in halves_scratch],
        compiler_params=pltpu.CompilerParams(vmem_limit_bytes=limit << 20),
        cost_estimate=pl.CostEstimate(flops=flops, bytes_accessed=4 * 10**6, transcendentals=0),
    )(*ins)


def exchange(x, axis):
    return lax.all_to_all(x, axis, 0, 0, tiled=True)


def shards(matrix, checksum, failed):
    core = lax.axis_index("core")
    p = lax.axis_index(ROW)
    q = lax.axis_index(COL)
    block = matrix.reshape(4608, 128)
    checks = checksum.reshape(3, 256, 3, 256).transpose(0, 2, 1, 3)
    core_arg = core.reshape(1).astype(jnp.int32)

    (col_send,) = call(prepare_kernel, [(16, 104, 256)], [block, failed], [VMEM, SMEM])
    col_got = exchange(col_send, COL)

    top_piece = [jnp.zeros((3, 16, 256), F32)] * PANELS
    for s in range(16):
        target = lax.rem(p + s, 16)
        part = lax.dynamic_slice_in_dim(checks[0], 16 * target, 16, 1)
        if s:
            part = lax.ppermute(part, ROW, [(k, (k + s) % 16) for k in range(PANELS)])
        source = lax.rem(p - s + 16, 16)
        top_piece = [jnp.where(source == k, part, top_piece[k]) for k in range(PANELS)]
    top_piece = jnp.concatenate(top_piece)
    col_got, top_piece = lax.optimization_barrier((col_got, top_piece))

    check_piece = lax.dynamic_slice_in_dim(checks, q * 16, 16, 2)
    panel, lost, lead_send = call(
        rebuild_kernel,
        [(9, 16, 256), (6, 16, 256), (16, 3, 16, 256)],
        [col_got, check_piece],
    )
    row_panel = lax.all_gather(panel, COL)
    lost_all = lax.all_gather(lost, COL)

    swap = [(i * 16 + j, j * 16 + i) for i in range(16) for j in range(16)]
    col_piece = lax.ppermute(panel, ROW + COL, swap)
    lead_rows = exchange(lead_send, ROW)
    lead_rows, col_piece = lax.optimization_barrier((lead_rows, col_piece))
    (half_send,) = call(
        lead_half_kernel, [(16, 6, 8, 256)], [core_arg, lead_rows[:PANELS]], [SMEM, VMEM]
    )
    lead_mine = exchange(half_send, COL)
    lead_other = lax.ppermute(lead_mine, "core", [(0, 1), (1, 0)])

    both = jnp.concatenate([col_piece, top_piece])
    both, lead_mine, row_panel = lax.optimization_barrier((both, lead_mine, row_panel))
    mine = exchange(jnp.broadcast_to(both[None], (8, *both.shape)), "xy")

    off, inv = call(
        lead_kernel,
        [(PANELS, 256, 256)] * 2,
        [core_arg, lead_mine, lead_other],
        [SMEM, VMEM, VMEM],
        [(6, 256, 256)],
        2 * 10**10,
    )

    mine, inv = lax.optimization_barrier((mine, inv))
    other = lax.ppermute(mine, "core", [(0, 1), (1, 0)])

    totals, x, x3, y3 = call(
        solve_kernel,
        [(3, 3, 256, 256)] * 2,
        [core_arg, row_panel, mine, other, checks, off, inv],
        [SMEM] + [VMEM] * 6,
        [(9, 256, 256)] * 2,
        3 * 10**9,
        halves_outs=[(3, 256, 2304)] * 2,
        halves_scratch=[(3, 2304, 256), (6, 256, 768)],
        limit=32,
    )

    missing = col_got[0, 96, 0].astype(jnp.int32)
    place = jnp.stack([p, q, missing]).astype(jnp.int32)
    (factored,) = call(
        finish_kernel,
        [(4608, 128)],
        [place, lost_all, block, x, x3, y3],
        [SMEM] + [VMEM] * 5,
    )
    totals = totals.transpose(0, 2, 1, 3).reshape(checksum.shape)
    return (factored.reshape(matrix.shape), totals)


def solution(mesh):
    finer = Mesh(mesh.devices.reshape(8, 2, 2, 8), ("xy", "core", "col_0", "col_1"))
    in_specs = (P(ROW, None, None, COL, None, None), P(ROW, None, None, None, None), P(COL))
    out_specs = (P(ROW, None, None, COL, None, None), P(ROW, None, None, None, None))
    return jax.shard_map(
        shards, mesh=finer, in_specs=in_specs, out_specs=out_specs, check_vma=False
    )
```

profile of v0, /device:TPU:30, one launch (start us, length us, event | category | flops | bytes accessed | tf_op | source)
XLA Modules:
  0.0 247.7 jit_solution(6491102524598751920)
XLA Ops:
  7.8 0.0 copy-start
  7.8 1.7 copy-done
  9.5 1.3 shard_map.50
  10.8 9.9 %all-to-all-start = ((f32[16,104,256]{2,1,0:T(8,128)}), f32[16,104,256]{2,1,0:T(8,128)S(1)}, u32[]{:S(2)}, u32[]{:S(2)}) async-start(f32[16,104,256]{2,1,0:T(8,128)} %shard_map.50), calls=%async_computation | async-start | bytes 3407872 | tf_op jit(solution)/shard_map/all_to_all | solution.py:305
  20.7 0.0 all-gather.7.cloned.1.call-start
  20.9 1.2 slice.9
  22.1 0.7 dynamic-slice_bitcast_fusion.1
  22.9 0.7 collective-permute-start.14
  23.5 0.7 collective-permute-start.13
  24.2 0.7 collective-permute-start.12
  24.9 0.7 collective-permute-start.11
  25.6 0.7 collective-permute-start.10
  26.2 0.7 collective-permute-start.9
  26.9 0.7 collective-permute-start.8
  27.6 0.7 collective-permute-start.7
  28.3 0.7 collective-permute-start.6
  29.0 0.7 collective-permute-start.5
  29.7 0.7 collective-permute-start.4
  30.3 1.3 collective-permute-start.3
  31.6 1.3 collective-permute-start.2
  33.0 1.3 collective-permute-start.1
  34.3 0.7 collective-permute-start
  34.9 0.9 dynamic-slice_bitcast_fusion.c_ref
  36.0 7.4 %collective-permute-done.3 = f32[3,16,256]{2,1,0:T(8,128)S(1)} collective-permute-done((f32[3,16,256]{2,1,0:T(8,128)}, f32[3,16,256]{2,1,0:T(8,128)S(1)}, u32[]{:S(2)}, u32[]{:S(2)}) %collective-permute-start.3) | collective-permute-done | bytes 49184 | tf_op jit(solution)/shard_map/ppermute | solution.py:324
  43.4 2.6 %collective-permute-done.2 = f32[3,16,256]{2,1,0:T(8,128)S(1)} collective-permute-done((f32[3,16,256]{2,1,0:T(8,128)S(1)}, f32[3,16,256]{2,1,0:T(8,128)S(1)}, u32[]{:S(2)}, u32[]{:S(2)}) %collective-permute-start.2) | collective-permute-done | bytes 49184 | tf_op jit(solution)/shard_map/ppermute | solution.py:324
  46.0 2.9 %collective-permute-done.1 = f32[3,16,256]{2,1,0:T(8,128)S(1)} collective-permute-done((f32[3,16,256]{2,1,0:T(8,128)S(1)}, f32[3,16,256]{2,1,0:T(8,128)S(1)}, u32[]{:S(2)}, u32[]{:S(2)}) %collective-permute-start.1) | collective-permute-done | bytes 49184 | tf_op jit(solution)/shard_map/ppermute | solution.py:324
  48.9 0.1 fusion.13
  48.9 0.1 fusion.27
  49.0 0.1 fusion.41
  49.2 10.7 %all-to-all-done.g_ref = f32[16,104,256]{2,1,0:T(8,128)S(1)} async-done(((f32[16,104,256]{2,1,0:T(8,128)}), f32[16,104,256]{2,1,0:T(8,128)S(1)}, u32[]{:S(2)}, u32[]{:S(2)}) %all-to-all-start) | async-done | bytes 1703968 | tf_op jit(solution)/shard_map/all_to_all | solution.py:305
  59.9 1.2 shard_map.51
  61.1 0.0 all-gather.7.cloned.1.call-update
  61.1 7.3 %all-to-all-start.1 = ((f32[16,3,16,256]{3,2,1,0:T(8,128)}), f32[16,3,16,256]{3,2,1,0:T(8,128)S(1)}, u32[]{:S(2)}, u32[]{:S(2)}) async-start(f32[16,3,16,256]{3,2,1,0:T(8,128)} %get-tuple-element.22), calls=%async_computation.1 | async-start | bytes 1572864 | tf_op jit(solution)/shard_map/all_to_all | solution.py:305
  68.4 5.7 %collective-permute-start.15 = (f32[9,16,256]{2,1,0:T(8,128)}, f32[9,16,256]{2,1,0:T(8,128)S(1)}, u32[]{:S(2)}, u32[]{:S(2)}) collective-permute-start(f32[9,16,256]{2,1,0:T(8,128)} %get-tuple-element.23), channel_id=1, source_target_pairs={{0,0},{1,16},{2,32},{3,48},{4,64},{5,80},{6,96},{7,112},{8,128},{9... | collective-permute-start | bytes 442376 | tf_op jit(solution)/shard_map/ppermute | solution.py:340
  74.1 15.0 %collective-permute-done.15 = f32[9,16,256]{2,1,0:T(8,128)S(1)} collective-permute-done((f32[9,16,256]{2,1,0:T(8,128)}, f32[9,16,256]{2,1,0:T(8,128)S(1)}, u32[]{:S(2)}, u32[]{:S(2)}) %collective-permute-start.15) | collective-permute-done | bytes 147488 | tf_op jit(solution)/shard_map/ppermute | solution.py:340
  89.1 0.1 shard_map.52
  89.2 0.6 copy-done.15
  89.8 33.3 %all_to_all.20.mine_ref = f32[16,6,8,256]{3,2,1,0:T(8,128)S(1)} all-to-all(f32[16,6,8,256]{3,2,1,0:T(8,128)S(1)} %shard_map.52), channel_id=1, replica_groups=mesh['xy'=8,'core'=2,'col_0'=2,'col_1'=8] {'col_0','col_1'}, dimensions={0} | all-to-all | bytes 1572864 | tf_op jit(solution)/shard_map/all_to_all | solution.py:305
  123.1 1.6 pad_maximum_fusion
  124.8 20.4 %all-gather.7.cloned.1.call-done = f32[144,16,256]{2,1,0:T(8,128)} async-done(((f32[9,16,256]{2,1,0:T(8,128)}), f32[144,16,256]{2,1,0:T(8,128)}) %all-gather.7.cloned.1.call-update) | async-done | bytes 2359312 | tf_op jit(solution)/shard_map/all_gather | solution.py:336
  145.2 2.7 %broadcast_in_dim.10 = f32[8,18,16,256]{3,2,1,0:T(8,128)} broadcast(f32[18,16,256]{2,1,0:T(8,128)} %pad_maximum_fusion), dimensions={1,2,3} | broadcast | bytes 2654208 | tf_op jit(solution)/shard_map/broadcast_in_dim | solution.py:351
  147.8 7.4 %all-to-all-start.3 = ((f32[8,18,16,256]{3,2,1,0:T(8,128)}), f32[8,18,16,256]{3,2,1,0:T(8,128)}, u32[]{:S(2)}, u32[]{:S(2)}) async-start(f32[8,18,16,256]{3,2,1,0:T(8,128)} %broadcast_in_dim.10), calls=%async_computation.3 | async-start | bytes 4718592 | tf_op jit(solution)/shard_map/all_to_all | solution.py:305
  155.2 0.7 all-gather.5.cloned.1.call-update
  156.0 29.2 %shard_map.53 = (f32[3,256,256]{2,1,0:T(8,128)S(1)}, f32[3,256,256]{2,1,0:T(8,128)S(1)}) custom-call(s32[1]{0:T(128)} %bitcast.27.core_ref, f32[16,6,8,256]{3,2,1,0:T(8,128)S(1)} %all_to_all.20.mine_ref, f32[16,6,8,256]{3,2,1,0:T(8,128)S(1)} %collective-permute-done.16.other_ref), custom_call_target="tpu_custom_call" | custom-call | flops 20000000000 | bytes 4000000 | tf_op jit(solution)/shard_map/pallas_call | solution.py:292
  185.2 0.0 copy-start.11
  185.2 0.9 copy-done.11
  186.0 0.9 copy-done.13
  187.0 0.5 slice.7
  188.1 0.1 pad_add_fusion.place_ref
  188.2 3.5 %collective-permute-done.17.other_ref = f32[8,18,16,256]{3,2,1,0:T(8,128)S(1)} collective-permute-done((f32[8,18,16,256]{3,2,1,0:T(8,128)}, f32[8,18,16,256]{3,2,1,0:T(8,128)S(1)}, u32[]{:S(2)}, u32[]{:S(2)}) %collective-permute-start.17) | collective-permute-done | bytes 2359328 | tf_op jit(solution)/shard_map/ppermute | solution.py:363
  191.7 1.7 copy-done.9
  193.4 1.7 copy-done.10
  195.1 1.1 copy-done.12
  196.2 1.1 copy-done.14
  197.4 21.9 %shard_map.54 = (f32[3,3,256,256]{3,2,1,0:T(8,128)}, f32[3,3,256,256]{3,2,1,0:T(8,128)S(1)}, bf16[3,256,2304]{2,1,0:T(8,128)(2,1)S(1)}, bf16[3,256,2304]{2,1,0:T(8,128)(2,1)S(1)}) custom-call(s32[1]{0:T(128)} %bitcast.27.core_ref, f32[16,9,16,256]{3,2,1,0:T(8,128)S(1)} %bitcast.143, f32[8,18,16,256]{3,2,1,0:T(8,128)} %all-to-all-done.3.mine_ref, ...), custom_call_target="tpu_custom_call" | custom-call | flops 3000000000 | bytes 4000000 | tf_op jit(solution)/shard_map/pallas_call | solution.py:292
  219.2 1.7 copy-done.2
  221.0 1.8 copy-done.4
  222.8 1.4 copy-done.6
  224.2 4.4 %all-gather.5.cloned.1.call-done = f32[96,16,256]{2,1,0:T(8,128)} async-done(((f32[6,16,256]{2,1,0:T(8,128)}), f32[96,16,256]{2,1,0:T(8,128)}) %all-gather.5.cloned.1.call-update) | async-done | bytes 1572880 | tf_op jit(solution)/shard_map/all_gather | solution.py:337
  228.6 2.0 copy-done.3
  230.6 2.0 copy-done.5
  232.6 1.7 copy-done.7
  234.2 1.4 copy-done.8
  235.6 5.2 %shard_map.55 = f32[4608,128]{1,0:T(8,128)} custom-call(s32[3]{0:T(128)S(1)} %pad_add_fusion.place_ref, f32[16,6,16,256]{3,2,1,0:T(8,128)S(1)} %bitcast.140, f32[4608,128]{1,0:T(8,128)S(1)} %bitcast.139, f32[3,3,256,256]{3,2,1,0:T(8,128)S(1)} %copy-done.7, bf16[3,256,2304]{2,1,0:T(8,128)(2,1)S(1)} %copy-done.3, bf16[3,256,2304]{2,1,0:T(8,128)(2,1)S(1)} %copy-done.5), custom_call_target="tpu_custom_call" | custom-call | flops 1000000 | bytes 4000000 | tf_op jit(solution)/shard_map/pallas_call | solution.py:292
  (35 shorter events, 0.1 us)
Async XLA Ops:
  7.8 1.7 copy-start
  10.8 49.1 %all-to-all-start = ((f32[16,104,256]{2,1,0:T(8,128)}), f32[16,104,256]{2,1,0:T(8,128)S(1)}, u32[]{:S(2)}, u32[]{:S(2)}) async-start(f32[16,104,256]{2,1,0:T(8,128)} %shard_map.50), calls=%async_computation | async-start | bytes 3407872 | tf_op jit(solution)/shard_map/all_to_all | solution.py:305
  20.7 124.4 %all-gather.7.cloned.1.call-start = ((), (), s32[]{:S(2)}) async-start(), calls=%async_computation.5 | async-start | bytes 2506752 | tf_op jit(solution)/shard_map/all_gather | solution.py:336
  22.9 3.3 %collective-permute-start.14 = (f32[3,16,256]{2,1,0:T(8,128)S(1)}, f32[3,16,256]{2,1,0:T(8,128)S(1)}, u32[]{:S(2)}, u32[]{:S(2)}) collective-permute-start(f32[3,16,256]{2,1,0:T(8,128)S(1)} %get-tuple-element.44), channel_id=1, source_target_pairs={{0,16},{16,32},{32,48},{1,17},{17,33},{33,49},{2,18},{18,34},{34,5... | collective-permute-start | bytes 147464 | tf_op jit(solution)/shard_map/ppermute | solution.py:324
  23.5 3.4 %collective-permute-start.13 = (f32[3,16,256]{2,1,0:T(8,128)S(1)}, f32[3,16,256]{2,1,0:T(8,128)S(1)}, u32[]{:S(2)}, u32[]{:S(2)}) collective-permute-start(f32[3,16,256]{2,1,0:T(8,128)S(1)} %get-tuple-element.45), channel_id=1, source_target_pairs={{0,32},{16,48},{32,64},{1,33},{17,49},{33,65},{2,34},{18,50},{34,6... | collective-permute-start | bytes 147464 | tf_op jit(solution)/shard_map/ppermute | solution.py:324
  24.2 3.4 %collective-permute-start.12 = (f32[3,16,256]{2,1,0:T(8,128)S(1)}, f32[3,16,256]{2,1,0:T(8,128)S(1)}, u32[]{:S(2)}, u32[]{:S(2)}) collective-permute-start(f32[3,16,256]{2,1,0:T(8,128)S(1)} %get-tuple-element.46), channel_id=1, source_target_pairs={{0,48},{16,64},{32,80},{1,49},{17,65},{33,81},{2,50},{18,66},{34,8... | collective-permute-start | bytes 147464 | tf_op jit(solution)/shard_map/ppermute | solution.py:324
  24.9 3.4 %collective-permute-start.11 = (f32[3,16,256]{2,1,0:T(8,128)S(1)}, f32[3,16,256]{2,1,0:T(8,128)S(1)}, u32[]{:S(2)}, u32[]{:S(2)}) collective-permute-start(f32[3,16,256]{2,1,0:T(8,128)S(1)} %get-tuple-element.47), channel_id=1, source_target_pairs={{0,64},{16,80},{32,96},{1,65},{17,81},{33,97},{2,66},{18,82},{34,9... | collective-permute-start | bytes 147464 | tf_op jit(solution)/shard_map/ppermute | solution.py:324
  25.6 3.4 %collective-permute-start.10 = (f32[3,16,256]{2,1,0:T(8,128)S(1)}, f32[3,16,256]{2,1,0:T(8,128)S(1)}, u32[]{:S(2)}, u32[]{:S(2)}) collective-permute-start(f32[3,16,256]{2,1,0:T(8,128)S(1)} %get-tuple-element.48), channel_id=1, source_target_pairs={{0,80},{16,96},{32,112},{1,81},{17,97},{33,113},{2,82},{18,98},{34... | collective-permute-start | bytes 147464 | tf_op jit(solution)/shard_map/ppermute | solution.py:324
  26.2 3.4 %collective-permute-start.9 = (f32[3,16,256]{2,1,0:T(8,128)S(1)}, f32[3,16,256]{2,1,0:T(8,128)S(1)}, u32[]{:S(2)}, u32[]{:S(2)}) collective-permute-start(f32[3,16,256]{2,1,0:T(8,128)S(1)} %get-tuple-element.49), channel_id=1, source_target_pairs={{0,96},{16,112},{32,128},{1,97},{17,113},{33,129},{2,98},{18,114},... | collective-permute-start | bytes 147464 | tf_op jit(solution)/shard_map/ppermute | solution.py:324
  26.9 3.4 %collective-permute-start.8 = (f32[3,16,256]{2,1,0:T(8,128)S(1)}, f32[3,16,256]{2,1,0:T(8,128)S(1)}, u32[]{:S(2)}, u32[]{:S(2)}) collective-permute-start(f32[3,16,256]{2,1,0:T(8,128)S(1)} %get-tuple-element.50), channel_id=1, source_target_pairs={{0,112},{16,128},{32,144},{1,113},{17,129},{33,145},{2,114},{18,13... | collective-permute-start | bytes 147464 | tf_op jit(solution)/shard_map/ppermute | solution.py:324
  27.6 4.0 %collective-permute-start.7 = (f32[3,16,256]{2,1,0:T(8,128)S(1)}, f32[3,16,256]{2,1,0:T(8,128)S(1)}, u32[]{:S(2)}, u32[]{:S(2)}) collective-permute-start(f32[3,16,256]{2,1,0:T(8,128)S(1)} %get-tuple-element.51), channel_id=1, source_target_pairs={{0,128},{16,144},{32,160},{1,129},{17,145},{33,161},{2,130},{18,14... | collective-permute-start | bytes 147464 | tf_op jit(solution)/shard_map/ppermute | solution.py:324
  28.3 4.7 %collective-permute-start.6 = (f32[3,16,256]{2,1,0:T(8,128)S(1)}, f32[3,16,256]{2,1,0:T(8,128)S(1)}, u32[]{:S(2)}, u32[]{:S(2)}) collective-permute-start(f32[3,16,256]{2,1,0:T(8,128)S(1)} %get-tuple-element.52), channel_id=1, source_target_pairs={{0,144},{16,160},{32,176},{1,145},{17,161},{33,177},{2,146},{18,16... | collective-permute-start | bytes 147464 | tf_op jit(solution)/shard_map/ppermute | solution.py:324
  29.0 5.3 %collective-permute-start.5 = (f32[3,16,256]{2,1,0:T(8,128)S(1)}, f32[3,16,256]{2,1,0:T(8,128)S(1)}, u32[]{:S(2)}, u32[]{:S(2)}) collective-permute-start(f32[3,16,256]{2,1,0:T(8,128)S(1)} %get-tuple-element.53), channel_id=1, source_target_pairs={{0,160},{16,176},{32,192},{1,161},{17,177},{33,193},{2,162},{18,17... | collective-permute-start | bytes 147464 | tf_op jit(solution)/shard_map/ppermute | solution.py:324
  29.7 6.4 %collective-permute-start.4 = (f32[3,16,256]{2,1,0:T(8,128)}, f32[3,16,256]{2,1,0:T(8,128)S(1)}, u32[]{:S(2)}, u32[]{:S(2)}) collective-permute-start(f32[3,16,256]{2,1,0:T(8,128)} %get-tuple-element.54), channel_id=1, source_target_pairs={{0,176},{16,192},{32,208},{1,177},{17,193},{33,209},{2,178},{18,19... | collective-permute-start | bytes 147464 | tf_op jit(solution)/shard_map/ppermute | solution.py:324
  30.3 13.1 %collective-permute-start.3 = (f32[3,16,256]{2,1,0:T(8,128)}, f32[3,16,256]{2,1,0:T(8,128)S(1)}, u32[]{:S(2)}, u32[]{:S(2)}) collective-permute-start(f32[3,16,256]{2,1,0:T(8,128)} %get-tuple-element.55), channel_id=1, source_target_pairs={{0,192},{16,208},{32,224},{1,193},{17,209},{33,225},{2,194},{18,21... | collective-permute-start | bytes 147464 | tf_op jit(solution)/shard_map/ppermute | solution.py:324
  31.6 14.4 %collective-permute-start.2 = (f32[3,16,256]{2,1,0:T(8,128)S(1)}, f32[3,16,256]{2,1,0:T(8,128)S(1)}, u32[]{:S(2)}, u32[]{:S(2)}) collective-permute-start(f32[3,16,256]{2,1,0:T(8,128)S(1)} %get-tuple-element.56), channel_id=1, source_target_pairs={{0,208},{16,224},{32,240},{1,209},{17,225},{33,241},{2,210},{18,22... | collective-permute-start | bytes 147464 | tf_op jit(solution)/shard_map/ppermute | solution.py:324
  33.0 15.9 %collective-permute-start.1 = (f32[3,16,256]{2,1,0:T(8,128)S(1)}, f32[3,16,256]{2,1,0:T(8,128)S(1)}, u32[]{:S(2)}, u32[]{:S(2)}) collective-permute-start(f32[3,16,256]{2,1,0:T(8,128)S(1)} %get-tuple-element.57), channel_id=1, source_target_pairs={{0,224},{16,240},{32,0},{1,225},{17,241},{33,1},{2,226},{18,242},{... | collective-permute-start | bytes 147464 | tf_op jit(solution)/shard_map/ppermute | solution.py:324
  34.3 14.6 %collective-permute-start = (f32[3,16,256]{2,1,0:T(8,128)S(1)}, f32[3,16,256]{2,1,0:T(8,128)S(1)}, u32[]{:S(2)}, u32[]{:S(2)}) collective-permute-start(f32[3,16,256]{2,1,0:T(8,128)S(1)} %get-tuple-element.58), channel_id=1, source_target_pairs={{0,240},{16,0},{32,16},{1,241},{17,1},{33,17},{2,242},{18,2},{34,1... | collective-permute-start | bytes 147464 | tf_op jit(solution)/shard_map/ppermute | solution.py:324
  61.1 28.0 %all-to-all-start.1 = ((f32[16,3,16,256]{3,2,1,0:T(8,128)}), f32[16,3,16,256]{3,2,1,0:T(8,128)S(1)}, u32[]{:S(2)}, u32[]{:S(2)}) async-start(f32[16,3,16,256]{3,2,1,0:T(8,128)} %get-tuple-element.22), calls=%async_computation.1 | async-start | bytes 1572864 | tf_op jit(solution)/shard_map/all_to_all | solution.py:305
  68.4 20.7 %collective-permute-start.15 = (f32[9,16,256]{2,1,0:T(8,128)}, f32[9,16,256]{2,1,0:T(8,128)S(1)}, u32[]{:S(2)}, u32[]{:S(2)}) collective-permute-start(f32[9,16,256]{2,1,0:T(8,128)} %get-tuple-element.23), channel_id=1, source_target_pairs={{0,0},{1,16},{2,32},{3,48},{4,64},{5,80},{6,96},{7,112},{8,128},{9... | collective-permute-start | bytes 442376 | tf_op jit(solution)/shard_map/ppermute | solution.py:340
  89.1 0.7 copy-start.15
  123.1 32.9 %collective-permute-start.16 = (f32[16,6,8,256]{3,2,1,0:T(8,128)S(1)}, f32[16,6,8,256]{3,2,1,0:T(8,128)S(1)}, u32[]{:S(2)}, u32[]{:S(2)}) collective-permute-start(f32[16,6,8,256]{3,2,1,0:T(8,128)S(1)} %all_to_all.20.mine_ref), channel_id=1, source_target_pairs={{0,16},{16,0},{1,17},{17,1},{2,18},{18,2},{3,19},{19,3},{4,20},{20... | collective-permute-start | bytes 2359304 | tf_op jit(solution)/shard_map/ppermute | solution.py:347
  147.8 39.2 %all-to-all-start.3 = ((f32[8,18,16,256]{3,2,1,0:T(8,128)}), f32[8,18,16,256]{3,2,1,0:T(8,128)}, u32[]{:S(2)}, u32[]{:S(2)}) async-start(f32[8,18,16,256]{3,2,1,0:T(8,128)} %broadcast_in_dim.10), calls=%async_computation.3 | async-start | bytes 4718592 | tf_op jit(solution)/shard_map/all_to_all | solution.py:305
  155.2 73.3 %all-gather.5.cloned.1.call-start = ((), (), s32[]{:S(2)}) async-start(), calls=%async_computation.4 | async-start | bytes 1671168 | tf_op jit(solution)/shard_map/all_gather | solution.py:337
  185.2 0.9 copy-start.11
  186.0 0.9 copy-start.13
  187.0 4.7 %collective-permute-start.17 = (f32[8,18,16,256]{3,2,1,0:T(8,128)}, f32[8,18,16,256]{3,2,1,0:T(8,128)S(1)}, u32[]{:S(2)}, u32[]{:S(2)}) collective-permute-start(f32[8,18,16,256]{3,2,1,0:T(8,128)} %all-to-all-done.3.mine_ref), channel_id=1, source_target_pairs={{0,16},{16,0},{1,17},{17,1},{2,18},{18,2},{3,19},{19,3},{4,20},{20... | collective-permute-start | bytes 7077896 | tf_op jit(solution)/shard_map/ppermute | solution.py:363
  191.7 1.7 copy-start.9
  193.4 1.7 copy-start.10
  195.1 1.1 copy-start.12
  196.2 1.1 copy-start.14
  197.4 31.2 %copy-start.1 = (f32[1,3,256,1,3,256]{5,3,4,2,1,0:T(1,128)S(1)}, f32[1,3,256,1,3,256]{5,3,4,2,1,0:T(1,128)}, u32[]{:S(2)}) copy-start(f32[1,3,256,1,3,256]{5,3,4,2,1,0:T(1,128)} %param.3) | copy-start | bytes 7077892
  219.2 1.8 copy-start.2
  221.0 1.8 copy-start.4
  222.8 1.4 copy-start.6
  228.6 2.0 copy-start.3
  230.6 2.0 copy-start.5
  232.6 1.7 copy-start.7
  234.2 1.4 copy-start.8
Sparse Core Ops, SparseCore 0:
  61.2 83.8 all-gather.6
  157.9 70.6 all-gather.4
where the time goes:
time: 249 us; the launch traced here: 248 us
  waiting for transfers between devices  67.6 us (27%)
  Pallas kernels  58.8 us (24%)
  starting transfers between devices  42.3 us (17%)
  blocking collectives  33.3 us (13%)
  local copies, waits for them, and re-layouts  27.7 us (11%)
  between operations  16 us (6%)
    pallas_call x6, Pallas kernels, call(): pl.pallas_call(kernel, out_shape=shapes, in_specs=specs or [VMEM] * len(i...  58.8 us
    all_to_all x1, blocking collectives, exchange(): return lax.all_to_all(x, axis, 0, 0, tiled=True)  33.3 us
    all_to_all x3, starting transfers between devices, exchange(): return lax.all_to_all(x, axis, 0, 0, tiled=True)  24.7 us
    unnamed x32, local copies, waits for them, and re-layouts  21.7 us
    all_gather x1, waiting for transfers between devices, shards(): row_panel = lax.all_gather(panel, COL)  20.4 us
    ppermute x1, waiting for transfers between devices, shards(): col_piece = lax.ppermute(panel, ROW + COL, swap)  15 us
    ppermute x15, waiting for transfers between devices, shards(): part = lax.ppermute(part, ROW, [(k, (k + s) % 16) for k in range(PANELS)])  12.9 us
    ppermute x15, starting transfers between devices, shards(): part = lax.ppermute(part, ROW, [(k, (k + s) % 16) for k in range(PANELS)])  11.8 us
  transfers between devices with their start and end apart: 23, of which 8 were waited for; matrix products, arithmetic and copies ran while one was open for 3% of the time, Pallas kernels for 21%

commit v1 on v0

--- a/solution.py
+++ b/solution.py
@@ -182,7 +182,7 @@
 
 def solve_kernel(
     core_ref, r_ref, mine_ref, other_ref, c_ref, off_ref, inv_ref,
-    t_ref, x_ref, x3_ref, y3_ref, q_ref, k_ref, s3_ref, w3_ref,
+    t_ref, x3_ref, y3_ref, q_ref, k_ref, s3_ref, w3_ref,
 ):
 
     def gather(even, odd):
@@ -208,8 +208,6 @@
     @pl.loop(0, 3)
     def _(a):
         xs, (x0_3, x1_3) = solve(lambda k: whole(r_ref, 3 * a + k))
-        for k in range(PANELS):
-            x_ref[a, k] = xs[k]
         x3_ref[a, :, 0:768] = x0_3
         x3_ref[a, :, 768:1536] = x1_3
         x3_ref[a, :, 1536:2304] = high_twice(xs[2], 1)
@@ -238,7 +236,7 @@
         t_ref[a, b] = c_ref[a, b] - dot3(x3_ref[a], s3_ref[b])
 
 
-def finish_kernel(place_ref, d_ref, m_ref, x_ref, x3_ref, y3_ref, f_ref):
+def finish_kernel(place_ref, d_ref, m_ref, x3_ref, y3_ref, f_ref):
     p, q, missing = place_ref[0], place_ref[1], place_ref[2]
 
     def store(a, b, value):
@@ -259,7 +257,9 @@
 
             @pl.when(panel)
             def _():
-                value = x_ref[a, jnp.minimum(q, PANELS - 1)]
+                start = pl.multiple_of(768 * jnp.minimum(q, PANELS - 1), 128)
+                value = x3_ref[a, :, pl.ds(start, 256)].astype(F32)
+                value = value + x3_ref[a, :, pl.ds(start + 512, 256)].astype(F32)
                 rows = lax.broadcasted_iota(jnp.int32, (256, 256), 0)
                 cols = lax.broadcasted_iota(jnp.int32, (256, 256), 1)
                 value = jnp.where(jnp.logical_or(rows >= cols, i > q), value, 0.0)
@@ -362,9 +362,9 @@
     mine, inv = lax.optimization_barrier((mine, inv))
     other = lax.ppermute(mine, "core", [(0, 1), (1, 0)])
 
-    totals, x, x3, y3 = call(
+    totals, x3, y3 = call(
         solve_kernel,
-        [(3, 3, 256, 256)] * 2,
+        [(3, 3, 256, 256)],
         [core_arg, row_panel, mine, other, checks, off, inv],
         [SMEM] + [VMEM] * 6,
         [(9, 256, 256)] * 2,
@@ -379,8 +379,8 @@
     (factored,) = call(
         finish_kernel,
         [(4608, 128)],
-        [place, lost_all, block, x, x3, y3],
-        [SMEM] + [VMEM] * 5,
+        [place, lost_all, block, x3, y3],
+        [SMEM] + [VMEM] * 4,
     )
     totals = totals.transpose(0, 2, 1, 3).reshape(checksum.shape)
     return (factored.reshape(matrix.shape), totals)

time: 249 us -> 247 us (level)
  local copies, waits for them, and re-layouts: 27.7 us -> 24.7 us
    unnamed x32 -> x28, local copies, waits for them, and re-layouts: 21.7 us -> 18.6 us
where the time goes in v1:
time: 247 us; the launch traced here: 246 us
  waiting for transfers between devices  69 us (28%)
  Pallas kernels  58.8 us (24%)
  starting transfers between devices  42.3 us (17%)
  blocking collectives  33.4 us (14%)
  local copies, waits for them, and re-layouts  24.7 us (10%)
  between operations  16 us (6%)
    pallas_call x6, Pallas kernels, call(): pl.pallas_call(kernel, out_shape=shapes, in_specs=specs or [VMEM] * len(i...  58.8 us
    all_to_all x1, blocking collectives, exchange(): return lax.all_to_all(x, axis, 0, 0, tiled=True)  33.4 us
    all_to_all x3, starting transfers between devices, exchange(): return lax.all_to_all(x, axis, 0, 0, tiled=True)  24.7 us
    all_gather x1, waiting for transfers between devices, shards(): row_panel = lax.all_gather(panel, COL)  20.4 us
    unnamed x28, local copies, waits for them, and re-layouts  18.6 us
    ppermute x1, waiting for transfers between devices, shards(): col_piece = lax.ppermute(panel, ROW + COL, swap)  15 us
    ppermute x15, waiting for transfers between devices, shards(): part = lax.ppermute(part, ROW, [(k, (k + s) % 16) for k in range(PANELS)])  12.9 us
    ppermute x15, starting transfers between devices, shards(): part = lax.ppermute(part, ROW, [(k, (k + s) % 16) for k in range(PANELS)])  11.8 us
  transfers between devices with their start and end apart: 23, of which 8 were waited for; matrix products, arithmetic and copies ran while one was open for 3% of the time, Pallas kernels for 21%

profile of v1, /device:TPU:30, one launch (start us, length us, event | category | flops | bytes accessed | tf_op | source)
XLA Modules:
  0.0 246.1 jit_solution(12642881669056914258)
XLA Ops:
  7.8 0.0 copy-start
  7.8 1.7 copy-done
  9.5 1.3 shard_map.50
  10.8 9.9 %all-to-all-start = ((f32[16,104,256]{2,1,0:T(8,128)}), f32[16,104,256]{2,1,0:T(8,128)S(1)}, u32[]{:S(2)}, u32[]{:S(2)}) async-start(f32[16,104,256]{2,1,0:T(8,128)} %shard_map.50), calls=%async_computation | async-start | bytes 3407872 | tf_op jit(solution)/shard_map/all_to_all | solution.py:305
  20.7 0.0 all-gather.7.cloned.1.call-start
  20.9 1.2 slice.9
  22.1 0.8 dynamic-slice_bitcast_fusion.1
  22.9 0.7 collective-permute-start.14
  23.5 0.7 collective-permute-start.13
  24.2 0.7 collective-permute-start.12
  24.9 0.7 collective-permute-start.11
  25.6 0.7 collective-permute-start.10
  26.2 0.0 collective-permute-done.14
  26.2 0.7 collective-permute-start.9
  26.9 0.7 collective-permute-start.8
  27.6 0.7 collective-permute-start.7
  28.3 0.0 collective-permute-done.11
  28.3 0.7 collective-permute-start.6
  29.0 0.7 collective-permute-start.5
  29.7 0.7 collective-permute-start.4
  30.3 1.3 collective-permute-start.3
  31.6 1.3 collective-permute-start.2
  33.0 1.3 collective-permute-start.1
  34.3 0.7 collective-permute-start
  34.9 0.9 dynamic-slice_bitcast_fusion.c_ref
  36.0 7.4 %collective-permute-done.3 = f32[3,16,256]{2,1,0:T(8,128)S(1)} collective-permute-done((f32[3,16,256]{2,1,0:T(8,128)}, f32[3,16,256]{2,1,0:T(8,128)S(1)}, u32[]{:S(2)}, u32[]{:S(2)}) %collective-permute-start.3) | collective-permute-done | bytes 49184 | tf_op jit(solution)/shard_map/ppermute | solution.py:324
  43.4 2.6 %collective-permute-done.2 = f32[3,16,256]{2,1,0:T(8,128)S(1)} collective-permute-done((f32[3,16,256]{2,1,0:T(8,128)S(1)}, f32[3,16,256]{2,1,0:T(8,128)S(1)}, u32[]{:S(2)}, u32[]{:S(2)}) %collective-permute-start.2) | collective-permute-done | bytes 49184 | tf_op jit(solution)/shard_map/ppermute | solution.py:324
  46.0 2.8 %collective-permute-done.1 = f32[3,16,256]{2,1,0:T(8,128)S(1)} collective-permute-done((f32[3,16,256]{2,1,0:T(8,128)S(1)}, f32[3,16,256]{2,1,0:T(8,128)S(1)}, u32[]{:S(2)}, u32[]{:S(2)}) %collective-permute-start.1) | collective-permute-done | bytes 49184 | tf_op jit(solution)/shard_map/ppermute | solution.py:324
  48.9 0.1 fusion.13
  48.9 0.1 fusion.27
  49.0 0.1 fusion.41
  49.2 10.7 %all-to-all-done.g_ref = f32[16,104,256]{2,1,0:T(8,128)S(1)} async-done(((f32[16,104,256]{2,1,0:T(8,128)}), f32[16,104,256]{2,1,0:T(8,128)S(1)}, u32[]{:S(2)}, u32[]{:S(2)}) %all-to-all-start) | async-done | bytes 1703968 | tf_op jit(solution)/shard_map/all_to_all | solution.py:305
  59.9 1.2 shard_map.51
  61.1 0.0 all-gather.7.cloned.1.call-update
  61.1 7.3 %all-to-all-start.1 = ((f32[16,3,16,256]{3,2,1,0:T(8,128)}), f32[16,3,16,256]{3,2,1,0:T(8,128)S(1)}, u32[]{:S(2)}, u32[]{:S(2)}) async-start(f32[16,3,16,256]{3,2,1,0:T(8,128)} %get-tuple-element.21), calls=%async_computation.1 | async-start | bytes 1572864 | tf_op jit(solution)/shard_map/all_to_all | solution.py:305
  68.4 5.7 %collective-permute-start.15 = (f32[9,16,256]{2,1,0:T(8,128)}, f32[9,16,256]{2,1,0:T(8,128)S(1)}, u32[]{:S(2)}, u32[]{:S(2)}) collective-permute-start(f32[9,16,256]{2,1,0:T(8,128)} %get-tuple-element.22), channel_id=1, source_target_pairs={{0,0},{1,16},{2,32},{3,48},{4,64},{5,80},{6,96},{7,112},{8,128},{9... | collective-permute-start | bytes 442376 | tf_op jit(solution)/shard_map/ppermute | solution.py:340
  74.1 15.0 %collective-permute-done.15 = f32[9,16,256]{2,1,0:T(8,128)S(1)} collective-permute-done((f32[9,16,256]{2,1,0:T(8,128)}, f32[9,16,256]{2,1,0:T(8,128)S(1)}, u32[]{:S(2)}, u32[]{:S(2)}) %collective-permute-start.15) | collective-permute-done | bytes 147488 | tf_op jit(solution)/shard_map/ppermute | solution.py:340
  89.1 0.1 shard_map.52
  89.2 0.6 copy-done.13
  89.8 33.4 %all_to_all.20.mine_ref = f32[16,6,8,256]{3,2,1,0:T(8,128)S(1)} all-to-all(f32[16,6,8,256]{3,2,1,0:T(8,128)S(1)} %shard_map.52), channel_id=1, replica_groups=mesh['xy'=8,'core'=2,'col_0'=2,'col_1'=8] {'col_0','col_1'}, dimensions={0} | all-to-all | bytes 1572864 | tf_op jit(solution)/shard_map/all_to_all | solution.py:305
  123.2 1.6 pad_maximum_fusion
  124.8 20.4 %all-gather.7.cloned.1.call-done = f32[144,16,256]{2,1,0:T(8,128)} async-done(((f32[9,16,256]{2,1,0:T(8,128)}), f32[144,16,256]{2,1,0:T(8,128)}) %all-gather.7.cloned.1.call-update) | async-done | bytes 2359312 | tf_op jit(solution)/shard_map/all_gather | solution.py:336
  145.2 2.7 %broadcast_in_dim.10 = f32[8,18,16,256]{3,2,1,0:T(8,128)} broadcast(f32[18,16,256]{2,1,0:T(8,128)} %pad_maximum_fusion), dimensions={1,2,3} | broadcast | bytes 2654208 | tf_op jit(solution)/shard_map/broadcast_in_dim | solution.py:351
  147.8 7.4 %all-to-all-start.3 = ((f32[8,18,16,256]{3,2,1,0:T(8,128)}), f32[8,18,16,256]{3,2,1,0:T(8,128)}, u32[]{:S(2)}, u32[]{:S(2)}) async-start(f32[8,18,16,256]{3,2,1,0:T(8,128)} %broadcast_in_dim.10), calls=%async_computation.3 | async-start | bytes 4718592 | tf_op jit(solution)/shard_map/all_to_all | solution.py:305
  155.3 0.7 all-gather.5.cloned.1.call-update
  156.0 29.2 %shard_map.53 = (f32[3,256,256]{2,1,0:T(8,128)S(1)}, f32[3,256,256]{2,1,0:T(8,128)S(1)}) custom-call(s32[1]{0:T(128)} %bitcast.27.core_ref, f32[16,6,8,256]{3,2,1,0:T(8,128)S(1)} %all_to_all.20.mine_ref, f32[16,6,8,256]{3,2,1,0:T(8,128)S(1)} %collective-permute-done.16.other_ref), custom_call_target="tpu_custom_call" | custom-call | flops 20000000000 | bytes 4000000 | tf_op jit(solution)/shard_map/pallas_call | solution.py:292
  185.2 0.0 copy-start.9
  185.2 0.9 copy-done.9
  186.1 0.9 copy-done.11
  187.0 0.5 slice.7
  188.2 0.1 pad_add_fusion.place_ref
  188.2 3.5 %collective-permute-done.17.other_ref = f32[8,18,16,256]{3,2,1,0:T(8,128)S(1)} collective-permute-done((f32[8,18,16,256]{3,2,1,0:T(8,128)}, f32[8,18,16,256]{3,2,1,0:T(8,128)S(1)}, u32[]{:S(2)}, u32[]{:S(2)}) %collective-permute-start.17) | collective-permute-done | bytes 2359328 | tf_op jit(solution)/shard_map/ppermute | solution.py:363
  191.7 1.7 copy-done.7
  193.4 1.7 copy-done.8
  195.1 1.1 copy-done.10
  196.2 1.1 copy-done.12
  197.4 21.8 %shard_map.54 = (f32[3,3,256,256]{3,2,1,0:T(8,128)}, bf16[3,256,2304]{2,1,0:T(8,128)(2,1)S(1)}, bf16[3,256,2304]{2,1,0:T(8,128)(2,1)S(1)}) custom-call(s32[1]{0:T(128)} %bitcast.27.core_ref, f32[16,9,16,256]{3,2,1,0:T(8,128)S(1)} %bitcast.143, f32[8,18,16,256]{3,2,1,0:T(8,128)} %all-to-all-done.3.mine_ref, ...), custom_call_target="tpu_custom_call" | custom-call | flops 3000000000 | bytes 4000000 | tf_op jit(solution)/shard_map/pallas_call | solution.py:292
  219.2 1.7 copy-done.2
  221.0 1.8 copy-done.4
  222.8 5.9 %all-gather.5.cloned.1.call-done = f32[96,16,256]{2,1,0:T(8,128)} async-done(((f32[6,16,256]{2,1,0:T(8,128)}), f32[96,16,256]{2,1,0:T(8,128)}) %all-gather.5.cloned.1.call-update) | async-done | bytes 1572880 | tf_op jit(solution)/shard_map/all_gather | solution.py:337
  228.6 2.0 copy-done.3
  230.6 2.0 copy-done.5
  232.6 1.4 copy-done.6
  234.0 5.2 %shard_map.55 = f32[4608,128]{1,0:T(8,128)} custom-call(s32[3]{0:T(128)S(1)} %pad_add_fusion.place_ref, f32[16,6,16,256]{3,2,1,0:T(8,128)S(1)} %bitcast.140, f32[4608,128]{1,0:T(8,128)S(1)} %bitcast.139, bf16[3,256,2304]{2,1,0:T(8,128)(2,1)S(1)} %copy-done.3, bf16[3,256,2304]{2,1,0:T(8,128)(2,1)S(1)} %copy-done.5), custom_call_target="tpu_custom_call" | custom-call | flops 1000000 | bytes 4000000 | tf_op jit(solution)/shard_map/pallas_call | solution.py:292
  (31 shorter events, 0.1 us)
Async XLA Ops:
  7.8 1.7 copy-start
  10.8 49.1 %all-to-all-start = ((f32[16,104,256]{2,1,0:T(8,128)}), f32[16,104,256]{2,1,0:T(8,128)S(1)}, u32[]{:S(2)}, u32[]{:S(2)}) async-start(f32[16,104,256]{2,1,0:T(8,128)} %shard_map.50), calls=%async_computation | async-start | bytes 3407872 | tf_op jit(solution)/shard_map/all_to_all | solution.py:305
  20.7 124.5 %all-gather.7.cloned.1.call-start = ((), (), s32[]{:S(2)}) async-start(), calls=%async_computation.5 | async-start | bytes 2506752 | tf_op jit(solution)/shard_map/all_gather | solution.py:336
  22.9 3.3 %collective-permute-start.14 = (f32[3,16,256]{2,1,0:T(8,128)S(1)}, f32[3,16,256]{2,1,0:T(8,128)S(1)}, u32[]{:S(2)}, u32[]{:S(2)}) collective-permute-start(f32[3,16,256]{2,1,0:T(8,128)S(1)} %get-tuple-element.42), channel_id=1, source_target_pairs={{0,16},{16,32},{32,48},{1,17},{17,33},{33,49},{2,18},{18,34},{34,5... | collective-permute-start | bytes 147464 | tf_op jit(solution)/shard_map/ppermute | solution.py:324
  23.5 3.4 %collective-permute-start.13 = (f32[3,16,256]{2,1,0:T(8,128)S(1)}, f32[3,16,256]{2,1,0:T(8,128)S(1)}, u32[]{:S(2)}, u32[]{:S(2)}) collective-permute-start(f32[3,16,256]{2,1,0:T(8,128)S(1)} %get-tuple-element.43), channel_id=1, source_target_pairs={{0,32},{16,48},{32,64},{1,33},{17,49},{33,65},{2,34},{18,50},{34,6... | collective-permute-start | bytes 147464 | tf_op jit(solution)/shard_map/ppermute | solution.py:324
  24.2 3.4 %collective-permute-start.12 = (f32[3,16,256]{2,1,0:T(8,128)S(1)}, f32[3,16,256]{2,1,0:T(8,128)S(1)}, u32[]{:S(2)}, u32[]{:S(2)}) collective-permute-start(f32[3,16,256]{2,1,0:T(8,128)S(1)} %get-tuple-element.44), channel_id=1, source_target_pairs={{0,48},{16,64},{32,80},{1,49},{17,65},{33,81},{2,50},{18,66},{34,8... | collective-permute-start | bytes 147464 | tf_op jit(solution)/shard_map/ppermute | solution.py:324
  24.9 3.4 %collective-permute-start.11 = (f32[3,16,256]{2,1,0:T(8,128)S(1)}, f32[3,16,256]{2,1,0:T(8,128)S(1)}, u32[]{:S(2)}, u32[]{:S(2)}) collective-permute-start(f32[3,16,256]{2,1,0:T(8,128)S(1)} %get-tuple-element.45), channel_id=1, source_target_pairs={{0,64},{16,80},{32,96},{1,65},{17,81},{33,97},{2,66},{18,82},{34,9... | collective-permute-start | bytes 147464 | tf_op jit(solution)/shard_map/ppermute | solution.py:324
  25.6 3.4 %collective-permute-start.10 = (f32[3,16,256]{2,1,0:T(8,128)S(1)}, f32[3,16,256]{2,1,0:T(8,128)S(1)}, u32[]{:S(2)}, u32[]{:S(2)}) collective-permute-start(f32[3,16,256]{2,1,0:T(8,128)S(1)} %get-tuple-element.46), channel_id=1, source_target_pairs={{0,80},{16,96},{32,112},{1,81},{17,97},{33,113},{2,82},{18,98},{34... | collective-permute-start | bytes 147464 | tf_op jit(solution)/shard_map/ppermute | solution.py:324
  26.2 3.4 %collective-permute-start.9 = (f32[3,16,256]{2,1,0:T(8,128)S(1)}, f32[3,16,256]{2,1,0:T(8,128)S(1)}, u32[]{:S(2)}, u32[]{:S(2)}) collective-permute-start(f32[3,16,256]{2,1,0:T(8,128)S(1)} %get-tuple-element.47), channel_id=1, source_target_pairs={{0,96},{16,112},{32,128},{1,97},{17,113},{33,129},{2,98},{18,114},... | collective-permute-start | bytes 147464 | tf_op jit(solution)/shard_map/ppermute | solution.py:324
  26.9 3.4 %collective-permute-start.8 = (f32[3,16,256]{2,1,0:T(8,128)S(1)}, f32[3,16,256]{2,1,0:T(8,128)S(1)}, u32[]{:S(2)}, u32[]{:S(2)}) collective-permute-start(f32[3,16,256]{2,1,0:T(8,128)S(1)} %get-tuple-element.48), channel_id=1, source_target_pairs={{0,112},{16,128},{32,144},{1,113},{17,129},{33,145},{2,114},{18,13... | collective-permute-start | bytes 147464 | tf_op jit(solution)/shard_map/ppermute | solution.py:324
  27.6 4.0 %collective-permute-start.7 = (f32[3,16,256]{2,1,0:T(8,128)S(1)}, f32[3,16,256]{2,1,0:T(8,128)S(1)}, u32[]{:S(2)}, u32[]{:S(2)}) collective-permute-start(f32[3,16,256]{2,1,0:T(8,128)S(1)} %get-tuple-element.49), channel_id=1, source_target_pairs={{0,128},{16,144},{32,160},{1,129},{17,145},{33,161},{2,130},{18,14... | collective-permute-start | bytes 147464 | tf_op jit(solution)/shard_map/ppermute | solution.py:324
  28.3 4.7 %collective-permute-start.6 = (f32[3,16,256]{2,1,0:T(8,128)S(1)}, f32[3,16,256]{2,1,0:T(8,128)S(1)}, u32[]{:S(2)}, u32[]{:S(2)}) collective-permute-start(f32[3,16,256]{2,1,0:T(8,128)S(1)} %get-tuple-element.50), channel_id=1, source_target_pairs={{0,144},{16,160},{32,176},{1,145},{17,161},{33,177},{2,146},{18,16... | collective-permute-start | bytes 147464 | tf_op jit(solution)/shard_map/ppermute | solution.py:324
  29.0 5.3 %collective-permute-start.5 = (f32[3,16,256]{2,1,0:T(8,128)S(1)}, f32[3,16,256]{2,1,0:T(8,128)S(1)}, u32[]{:S(2)}, u32[]{:S(2)}) collective-permute-start(f32[3,16,256]{2,1,0:T(8,128)S(1)} %get-tuple-element.51), channel_id=1, source_target_pairs={{0,160},{16,176},{32,192},{1,161},{17,177},{33,193},{2,162},{18,17... | collective-permute-start | bytes 147464 | tf_op jit(solution)/shard_map/ppermute | solution.py:324
  29.7 6.4 %collective-permute-start.4 = (f32[3,16,256]{2,1,0:T(8,128)}, f32[3,16,256]{2,1,0:T(8,128)S(1)}, u32[]{:S(2)}, u32[]{:S(2)}) collective-permute-start(f32[3,16,256]{2,1,0:T(8,128)} %get-tuple-element.52), channel_id=1, source_target_pairs={{0,176},{16,192},{32,208},{1,177},{17,193},{33,209},{2,178},{18,19... | collective-permute-start | bytes 147464 | tf_op jit(solution)/shard_map/ppermute | solution.py:324
  30.3 13.1 %collective-permute-start.3 = (f32[3,16,256]{2,1,0:T(8,128)}, f32[3,16,256]{2,1,0:T(8,128)S(1)}, u32[]{:S(2)}, u32[]{:S(2)}) collective-permute-start(f32[3,16,256]{2,1,0:T(8,128)} %get-tuple-element.53), channel_id=1, source_target_pairs={{0,192},{16,208},{32,224},{1,193},{17,209},{33,225},{2,194},{18,21... | collective-permute-start | bytes 147464 | tf_op jit(solution)/shard_map/ppermute | solution.py:324
  31.6 14.4 %collective-permute-start.2 = (f32[3,16,256]{2,1,0:T(8,128)S(1)}, f32[3,16,256]{2,1,0:T(8,128)S(1)}, u32[]{:S(2)}, u32[]{:S(2)}) collective-permute-start(f32[3,16,256]{2,1,0:T(8,128)S(1)} %get-tuple-element.54), channel_id=1, source_target_pairs={{0,208},{16,224},{32,240},{1,209},{17,225},{33,241},{2,210},{18,22... | collective-permute-start | bytes 147464 | tf_op jit(solution)/shard_map/ppermute | solution.py:324
  33.0 15.9 %collective-permute-start.1 = (f32[3,16,256]{2,1,0:T(8,128)S(1)}, f32[3,16,256]{2,1,0:T(8,128)S(1)}, u32[]{:S(2)}, u32[]{:S(2)}) collective-permute-start(f32[3,16,256]{2,1,0:T(8,128)S(1)} %get-tuple-element.55), channel_id=1, source_target_pairs={{0,224},{16,240},{32,0},{1,225},{17,241},{33,1},{2,226},{18,242},{... | collective-permute-start | bytes 147464 | tf_op jit(solution)/shard_map/ppermute | solution.py:324
  34.3 14.6 %collective-permute-start = (f32[3,16,256]{2,1,0:T(8,128)S(1)}, f32[3,16,256]{2,1,0:T(8,128)S(1)}, u32[]{:S(2)}, u32[]{:S(2)}) collective-permute-start(f32[3,16,256]{2,1,0:T(8,128)S(1)} %get-tuple-element.56), channel_id=1, source_target_pairs={{0,240},{16,0},{32,16},{1,241},{17,1},{33,17},{2,242},{18,2},{34,1... | collective-permute-start | bytes 147464 | tf_op jit(solution)/shard_map/ppermute | solution.py:324
  61.1 28.0 %all-to-all-start.1 = ((f32[16,3,16,256]{3,2,1,0:T(8,128)}), f32[16,3,16,256]{3,2,1,0:T(8,128)S(1)}, u32[]{:S(2)}, u32[]{:S(2)}) async-start(f32[16,3,16,256]{3,2,1,0:T(8,128)} %get-tuple-element.21), calls=%async_computation.1 | async-start | bytes 1572864 | tf_op jit(solution)/shard_map/all_to_all | solution.py:305
  68.4 20.7 %collective-permute-start.15 = (f32[9,16,256]{2,1,0:T(8,128)}, f32[9,16,256]{2,1,0:T(8,128)S(1)}, u32[]{:S(2)}, u32[]{:S(2)}) collective-permute-start(f32[9,16,256]{2,1,0:T(8,128)} %get-tuple-element.22), channel_id=1, source_target_pairs={{0,0},{1,16},{2,32},{3,48},{4,64},{5,80},{6,96},{7,112},{8,128},{9... | collective-permute-start | bytes 442376 | tf_op jit(solution)/shard_map/ppermute | solution.py:340
  89.1 0.7 copy-start.13
  123.2 32.8 %collective-permute-start.16 = (f32[16,6,8,256]{3,2,1,0:T(8,128)S(1)}, f32[16,6,8,256]{3,2,1,0:T(8,128)S(1)}, u32[]{:S(2)}, u32[]{:S(2)}) collective-permute-start(f32[16,6,8,256]{3,2,1,0:T(8,128)S(1)} %all_to_all.20.mine_ref), channel_id=1, source_target_pairs={{0,16},{16,0},{1,17},{17,1},{2,18},{18,2},{3,19},{19,3},{4,20},{20... | collective-permute-start | bytes 2359304 | tf_op jit(solution)/shard_map/ppermute | solution.py:347
  147.8 39.2 %all-to-all-start.3 = ((f32[8,18,16,256]{3,2,1,0:T(8,128)}), f32[8,18,16,256]{3,2,1,0:T(8,128)}, u32[]{:S(2)}, u32[]{:S(2)}) async-start(f32[8,18,16,256]{3,2,1,0:T(8,128)} %broadcast_in_dim.10), calls=%async_computation.3 | async-start | bytes 4718592 | tf_op jit(solution)/shard_map/all_to_all | solution.py:305
  155.3 73.4 %all-gather.5.cloned.1.call-start = ((), (), s32[]{:S(2)}) async-start(), calls=%async_computation.4 | async-start | bytes 1671168 | tf_op jit(solution)/shard_map/all_gather | solution.py:337
  185.2 0.9 copy-start.9
  186.1 0.9 copy-start.11
  187.0 4.7 %collective-permute-start.17 = (f32[8,18,16,256]{3,2,1,0:T(8,128)}, f32[8,18,16,256]{3,2,1,0:T(8,128)S(1)}, u32[]{:S(2)}, u32[]{:S(2)}) collective-permute-start(f32[8,18,16,256]{3,2,1,0:T(8,128)} %all-to-all-done.3.mine_ref), channel_id=1, source_target_pairs={{0,16},{16,0},{1,17},{17,1},{2,18},{18,2},{3,19},{19,3},{4,20},{20... | collective-permute-start | bytes 7077896 | tf_op jit(solution)/shard_map/ppermute | solution.py:363
  191.7 1.7 copy-start.7
  193.4 1.7 copy-start.8
  195.1 1.1 copy-start.10
  196.2 1.1 copy-start.12
  197.4 31.3 %copy-start.1 = (f32[1,3,256,1,3,256]{5,3,4,2,1,0:T(1,128)S(1)}, f32[1,3,256,1,3,256]{5,3,4,2,1,0:T(1,128)}, u32[]{:S(2)}) copy-start(f32[1,3,256,1,3,256]{5,3,4,2,1,0:T(1,128)} %param.3) | copy-start | bytes 7077892
  219.2 1.7 copy-start.2
  221.0 1.8 copy-start.4
  228.6 2.0 copy-start.3
  230.6 2.0 copy-start.5
  232.6 1.4 copy-start.6
Sparse Core Ops, SparseCore 0:
  61.2 83.9 all-gather.6
  157.9 70.7 all-gather.4
